TPU v7x, 256 devices: a whole 4x4x8 slice. The times are simulated.
256 devices in a mesh: chan: 16 (over z, core), blk: 8 (over y, x_lo), grid: 2 (over x_hi).
Axes of the slice: x: 4 (x_hi: 2, x_lo: 2; x = x_hi * 2 + x_lo), y: 4, z: 8, core: 2. Of those that a mesh axis runs over, the one named last changes fastest.
Arguments:
- samples: bfloat16 [2, 256, 262144], P('grid', 'blk', 'chan'), may hold values from -6 to 6
- pfb_taps: bfloat16 [4, 2048], replicated, may hold values from -0.09375 to 0.09375
- chan_select: int32 [1024], replicated, may hold values from 0 to 1023, each once
Outputs:
- visibility: float32 [2, 1024, 2, 256, 512], P(None, 'chan', None, 'blk', 'grid')
Inputs may be any that keep to these rules, and one draw needn't show every extreme that they name: chan_select holds every bin of 0 to 1023 once.
All inputs are finite; a program needn't handle non-finite values.
Results may differ from a plain program's by a relative error of at most 0.0059.
Values may be sent and summed in bfloat16 or wider, within the bound.
A program may use at most 128 MiB of HBM per device.

v0:
```python
import math

import jax
import jax.numpy as jnp
from jax import lax
from jax.sharding import PartitionSpec as P


def passed_along(block, axis, distance):
    devices = range(lax.axis_size(axis))
    route = [(i - distance, i) for i in devices if i - distance in devices]
    return lax.ppermute(block, axis, route)


def cross_products(columns, row_piece, spectra_count):
    group_size = columns.shape[3]
    count_a = columns.shape[0]
    count_i = row_piece.shape[0]
    left_side = columns.transpose(3, 0, 2, 1).reshape(group_size, count_a, 2 * spectra_count)
    real_part = row_piece[:, :, 0]
    imag_part = row_piece[:, :, 1]
    right_real = jnp.stack([real_part, imag_part], 1)
    right_imag = jnp.stack([-imag_part, real_part], 1)
    right_side = jnp.concatenate([right_real, right_imag], 0)
    right_side = right_side.transpose(3, 1, 2, 0).reshape(
        group_size, 2 * spectra_count, 2 * count_i
    )
    products = jnp.einsum("cak,ckb->cab", left_side, right_side, preferred_element_type=jnp.float32)
    products = products * (1.0 / spectra_count)
    return jnp.stack([products[:, :, :count_i], products[:, :, count_i:]])


def body(samples, pfb_taps, chan_select):
    taps_count, fft_length = pfb_taps.shape
    chan_count = lax.axis_size("chan")
    blk_count = lax.axis_size("blk")
    grid_count = lax.axis_size("grid")
    local = samples[0]
    inputs_dev = local.shape[0]
    spec_dev = local.shape[1] // fft_length
    history = passed_along(local[:, local.shape[1] - (taps_count - 1) * fft_length :], "chan", 1)
    joined = jnp.concatenate([history, local], 1).reshape(
        inputs_dev, spec_dev + taps_count - 1, fft_length
    )
    filtered = jnp.zeros((inputs_dev, spec_dev, fft_length), jnp.float32)
    for tap_index in range(taps_count):
        filtered = filtered + pfb_taps[tap_index].astype(jnp.float32) * joined[
            :, tap_index : tap_index + spec_dev
        ].astype(jnp.float32)
    filtered = filtered.astype(jnp.bfloat16)
    channels = chan_select.shape[0]
    group_size = channels // chan_count
    positions = jnp.arange(fft_length, dtype=jnp.int32)
    selected = chan_select.reshape(chan_count, group_size)
    phase_index = positions[:, None, None] * selected[None] % fft_length
    angles = phase_index.astype(jnp.float32) * (2.0 * math.pi / fft_length)
    dft_table = jnp.stack([jnp.cos(angles), -jnp.sin(angles)], 2).astype(jnp.bfloat16)
    dft_table = dft_table.reshape(fft_length, 2 * channels)
    spectra = jnp.dot(
        filtered.reshape(inputs_dev * spec_dev, fft_length),
        dft_table,
        preferred_element_type=jnp.float32,
    )
    spectra = spectra.astype(jnp.bfloat16).reshape(inputs_dev, spec_dev, chan_count, 2 * group_size)
    turned = lax.all_to_all(spectra, "chan", split_axis=2, concat_axis=1, tiled=True)
    spectra_count = turned.shape[1]
    turned = turned.reshape(inputs_dev, spectra_count, 2, group_size)
    gathered = lax.all_gather(turned, ("blk", "grid"), axis=0, tiled=True)
    gathered = gathered.reshape(blk_count, grid_count, inputs_dev, spectra_count, 2, group_size)
    row_block = lax.dynamic_index_in_dim(gathered, lax.axis_index("grid"), 1, False)
    row_block = row_block.reshape(blk_count * inputs_dev, spectra_count, 2, group_size)
    columns = lax.dynamic_index_in_dim(gathered, lax.axis_index("blk"), 0, False)
    columns = columns.reshape(grid_count * inputs_dev, spectra_count, 2, group_size)
    result = cross_products(columns, row_block, spectra_count)
    return result.reshape(2, group_size, grid_count, inputs_dev, result.shape[3])


def solution(mesh):
    return jax.shard_map(
        body,
        mesh=mesh,
        in_specs=(P("grid", "blk", "chan"), P(), P()),
        out_specs=P(None, "chan", None, "blk", "grid"),
        check_vma=False,
    )
```

profile of v0, /device:TPU:1, one launch (start us, length us, event | category | flops | bytes accessed | tf_op | source)
XLA Modules:
  0.0 545.8 jit_solution(13861194421789603010)
XLA Ops:
  6.5 0.0 all-gather.2.cloned.1.call-start
  6.5 1.0 slice.52
  7.6 4.9 collective-permute-start
  12.5 0.8 mul.90
  13.3 1.5 slice_convert_fusion.3
  14.8 35.4 %cosine_convert_fusion = (bf16[2048,16,1,64]{0,3,2,1:T(8,128)(2,1)S(1)}, bf16[2048,16,1,64]{0,3,2,1:T(8,128)(2,1)}) fusion(s32[16,64]{1,0:T(8,128)S(1)} %mul.90), kind=kLoop, calls=%fused_computation.10 | loop fusion | flops 35651584 | bytes 8392704 | tf_op jit(solution)/shard_map/convert.4
  50.1 0.0 copy-start.1
  50.1 6.4 %pad_maximum_fusion = bf16[2048,16,2,64]{0,3,2,1:T(8,128)(2,1)} fusion(bf16[2048,16,1,64]{0,3,2,1:T(8,128)(2,1)} %get-tuple-element.14, bf16[2048,16,1,64]{0,3,2,1:T(8,128)(2,1)S(1)} %get-tuple-element.13), kind=kLoop, calls=%fused_computation.7 | loop fusion | flops 4194304 | bytes 16777216 | tf_op jit(solution)/shard_map/stack | solution.py:57
  56.6 0.0 collective-permute-done
  56.6 0.0 copy-done.1
  56.6 0.1 pad_maximum_fusion.2
  56.7 1.0 reshape.137
  57.7 6.4 %fusion.6 = bf16[32,8,16,128]{3,1,2,0:T(8,128)(2,1)S(1)} fusion(bf16[2048,2048]{0,1:T(8,128)(2,1)} %bitcast.44, bf16[32,11,2048]{2,1,0:T(8,128)(2,1)S(1)} %reshape.137, f32[2048]{0:T(1024)} %bitcast.53, f32[2048]{0:T(1024)} %bitcast.54, f32[2048]{0:T(1024)S(1)} %bitcast.52, f32[2048]{0:T(1024)S(1)} %bitcast.51), kind=kOutput, calls=%fused_computation.20 | convolution fusion | flops 2154299392 | bytes 13664256 | tf_op jit(solution)/shard_map/dot_general | solution.py:59
  64.1 0.3 copy.15
  64.3 36.0 %all_to_all.15 = bf16[32,8,16,128]{3,1,0,2:T(8,128)(2,1)S(1)} all-to-all(bf16[32,8,16,128]{3,1,0,2:T(8,128)(2,1)S(1)} %copy.15), channel_id=1, replica_groups=mesh['chan'=16,'blk'=8,'grid'=2] {'chan'}, dimensions={2} | all-to-all | bytes 2097152 | tf_op jit(solution)/shard_map/all_to_all | solution.py:65
  100.4 0.3 copy.16
  100.7 0.8 reshape.140
  101.5 3.8 copy.17
  105.3 0.0 all-gather.2.cloned.1.call-update
  105.3 351.3 %all-gather.2.cloned.1.call-done = bf16[512,128,2,64]{1,3,2,0:T(8,128)(2,1)} async-done(((bf16[32,128,2,64]{1,3,2,0:T(8,128)(2,1)}), bf16[512,128,2,64]{1,3,2,0:T(8,128)(2,1)}) %all-gather.2.cloned.1.call-update) | async-done | bytes 16777232 | tf_op jit(solution)/shard_map/all_gather | solution.py:68
  456.7 10.8 %constant_dynamic-slice_fusion = bf16[8,1,32,128,2,64]{3,5,4,2,1,0:T(8,128)(2,1)} fusion(bf16[8,2,32,128,2,64]{3,5,4,2,1,0:T(8,128)(2,1)} %bitcast.46, s32[]{:T(128)S(6)} %select_n.28), kind=kLoop, calls=%fused_computation.34 | loop fusion | bytes 16777220 | tf_op jit(solution)/shard_map/jit(dynamic_index_in_dim)/dynamic_slice | solution.py:70
  467.4 0.0 copy-start
  467.5 5.0 fusion.17
  472.5 1.1 copy-done
  473.6 4.3 slice_bitcast_fusion
  477.9 1.8 constant_dynamic-slice_fusion.1
  479.7 3.5 copy.18
  483.2 3.2 reshape.143
  486.3 14.0 %maximum_bitcast_fusion = bf16[64,2,128,512]{2,0,3,1:T(8,128)(2,1)} fusion(bf16[256,1,128,64]{2,3,0,1:T(8,128)(2,1)} %get-tuple-element.8, bf16[256,1,128,64]{2,3,0,1:T(8,128)(2,1)} %fusion.17, bf16[256,1,128,64]{2,3,0,1:T(8,128)(2,1)} %get-tuple-element.7), kind=kLoop, calls=%fused_computation | loop fusion | flops 25165824 | bytes 29360128 | tf_op jit(solution)/shard_map/transpose | solution.py:25
  500.3 24.3 %copy.20 = bf16[64,2,128,512]{3,2,1,0:T(8,128)(2,1)} copy(bf16[64,2,128,512]{2,0,3,1:T(8,128)(2,1)} %maximum_bitcast_fusion) | data formatting | bytes 33554432 | tf_op jit(solution)/shard_map/transpose | solution.py:25
  524.6 8.8 %broadcast_multiply_fusion = f32[64,64,512]{2,1,0:T(8,128)S(1)} fusion(bf16[64,64,256]{2,1,0:T(8,128)(2,1)S(1)} %reshape.143, bf16[64,256,512]{2,1,0:T(8,128)(2,1)} %bitcast.39), kind=kOutput, calls=%fused_computation.16 | convolution fusion | flops 1075838976 | bytes 27262976 | tf_op jit(solution)/shard_map/cak,ckb->cab/dot_general | solution.py:28
  533.4 1.3 fusion.18
  534.7 4.3 pad_maximum_fusion.1
Async XLA Ops:
  6.5 450.1 %all-gather.2.cloned.1.call-start = ((), (), s32[]{:S(2)}) async-start(), calls=%async_computation.1 | async-start | bytes 17825792 | tf_op jit(solution)/shard_map/all_gather | solution.py:68
  7.6 49.0 %collective-permute-start = (bf16[32,6144]{1,0:T(8,128)(2,1)S(1)}, bf16[32,6144]{1,0:T(8,128)(2,1)S(1)}, u32[]{:S(2)}, u32[]{:S(2)}) collective-permute-start(bf16[32,6144]{1,0:T(8,128)(2,1)S(1)} %slice.52), channel_id=1, source_target_pairs={{0,16},{16,32},{32,48},{48,64},{64,80},{80,96},{96,112},{112,128},... | collective-permute-start | bytes 1179656 | tf_op jit(solution)/shard_map/ppermute | solution.py:12
  50.1 6.5 %copy-start.1 = (bf16[1,32,16384]{2,1,0:T(8,128)(2,1)S(1)}, bf16[1,32,16384]{2,1,0:T(8,128)(2,1)}, u32[]{:S(2)}) copy-start(bf16[1,32,16384]{2,1,0:T(8,128)(2,1)} %param.3) | copy-start | bytes 3145732
  467.4 6.2 %copy-start = (bf16[8,1,32,128,2,64]{3,5,4,2,1,0:T(8,128)(2,1)S(1)}, bf16[8,1,32,128,2,64]{3,5,4,2,1,0:T(8,128)(2,1)}, u32[]{:S(2)}) copy-start(bf16[8,1,32,128,2,64]{3,5,4,2,1,0:T(8,128)(2,1)} %constant_dynamic-slice_fusion) | copy-start | bytes 25165828
Sparse Core Ops, SparseCore 0:
  105.5 351.1 all-gather.1
where the time goes:
time: 547 us; the launch traced here: 546 us
  waiting for transfers between devices  351 us (64%)
  other arithmetic  66.7 us (12%)
  local copies, waits for them, and re-layouts  58.1 us (11%)
  blocking collectives  36 us (7%)
  matrix products  15.2 us (3%)
  between operations  13.5 us (2%)
    all_gather x1, waiting for transfers between devices, body(): gathered = lax.all_gather(turned, ('blk', 'grid'), axis=0, tiled=True)  351 us
    all_to_all x1, blocking collectives, body(): lax.all_to_all(spectra, 'chan', split_axis=2, concat_axis=1, tiled=True)  36 us
    another operation x1, other arithmetic  35.4 us
    transpose x1, local copies, waits for them, and re-layouts, cross_products(): right_side.transpose(3, 1, 2, 0)  24.3 us
    transpose x1, other arithmetic, cross_products(): right_side.transpose(3, 1, 2, 0)  14 us
  transfers between devices with their start and end apart: 2, of which 1 were waited for; matrix products, arithmetic and copies ran while one was open for 8% of the time, Pallas kernels for 0%

commit v1 on v0

v1 whole, which is shorter than its diff:
```python
import math

import jax
import jax.numpy as jnp
from jax import lax
from jax.experimental import pallas as pl
from jax.experimental.pallas import tpu as pltpu
from jax.sharding import PartitionSpec as P

MESH = pl.DeviceIdType.MESH
BF16 = jnp.bfloat16
F32 = jnp.float32
VMEM_LIMIT = 52 * 1024 * 1024

FFT = 2048
TAPS = 4
INPUTS = 32
FRAMES = 8
GROUP = 64
SHARDS = 16
SPECTRA = SHARDS * FRAMES
LANES = 2 * GROUP
HALO = (TAPS - 1) * FFT
COARSE, MIDDLE, FINE = 8, 16, 16
PIECES = 16
PIECE = GROUP // PIECES


def phase_tables(chan_select):
    bins = jnp.broadcast_to(chan_select.reshape(SHARDS, 1, GROUP), (SHARDS, 2, GROUP)).reshape(1, -1)
    quarter = (jnp.arange(SHARDS * LANES, dtype=jnp.int32) // GROUP % 2 * (FFT // 4)).reshape(1, -1)
    rows = jnp.arange(COARSE + MIDDLE + FINE, dtype=jnp.int32).reshape(-1, 1)
    is_coarse = rows < COARSE
    is_middle = rows < COARSE + MIDDLE
    step = jnp.where(is_coarse, rows * 256, jnp.where(is_middle, (rows - COARSE) * 16, rows - COARSE - MIDDLE))
    phase = (step * bins + jnp.where(is_middle, 0, quarter)) % FFT
    angle = phase.astype(F32) * (2.0 * math.pi / FFT)
    return jnp.cos(angle), jnp.sin(angle)


def spectra_kernel(
    samples, taps, cos_ref, sin_ref, out, frames, filt, table, fine_cos, fine_sin, sent, landed,
    spread, turned_re, turned_im, load_sem, halo_sems, send_sems, recv_sems,
):
    me = lax.axis_index("chan")
    my_z, my_core = me // 2, me % 2

    load = pltpu.make_async_copy(samples, frames.at[:, pl.ds(HALO, FRAMES * FFT)], load_sem)
    load.start()

    barrier = pltpu.get_barrier_semaphore()

    def greet(offset, carry):
        pl.semaphore_signal(barrier, inc=1, device_id={"chan": lax.rem(me + offset, SHARDS)}, device_id_type=MESH)
        return carry

    lax.fori_loop(1, SHARDS, greet, 0)
    pl.semaphore_wait(barrier, SHARDS - 1)

    halo = pltpu.make_async_remote_copy(
        src_ref=samples.at[:, pl.ds((FRAMES - TAPS + 1) * FFT, HALO)],
        dst_ref=frames.at[:, pl.ds(0, HALO)],
        send_sem=halo_sems.at[0],
        recv_sem=halo_sems.at[1],
        device_id={"chan": lax.rem(me + 1, SHARDS)},
        device_id_type=MESH,
    )
    halo.start()
    load.wait()

    width = 512

    def filter_frame(s):
        def part(i, carry):
            lanes = pl.multiple_of(i * width, width)
            total = jnp.zeros((INPUTS, width), F32)
            for t in range(TAPS):
                weight = taps[pl.ds(t, 1), pl.ds(lanes, width)].astype(F32)
                total = total + weight * frames[:, pl.ds((s + t) * FFT + lanes, width)].astype(F32)
            filt[pl.ds(s * INPUTS, INPUTS), pl.ds(lanes, width)] = total.astype(BF16)
            return carry

        lax.fori_loop(0, FFT // width, part, 0)

    for s in range(TAPS - 1, FRAMES):
        filter_frame(s)

    halo.wait_send()
    halo.wait_recv()

    @pl.when(me == 0)
    def _():
        frames[:, pl.ds(0, HALO)] = jnp.zeros((INPUTS, HALO), BF16)

    for s in range(TAPS - 1):
        filter_frame(s)

    def send(group):
        return pltpu.make_async_remote_copy(
            src_ref=sent.at[group],
            dst_ref=landed.at[me],
            send_sem=send_sems.at[group],
            recv_sem=recv_sems.at[me],
            device_id={"chan": group},
            device_id_type=MESH,
        )

    def transform(i, carry):
        away = 4 + (i + 1) // 2 * (1 - 2 * (i % 2))
        to_z = lax.rem(my_z + away, SHARDS // 2)
        lanes = pl.ds(pl.multiple_of(to_z * 2 * LANES, 2 * LANES), 2 * LANES)
        for u in range(MIDDLE):
            cos_u, sin_u = cos_ref[pl.ds(COARSE + u, 1), lanes], sin_ref[pl.ds(COARSE + u, 1), lanes]
            cos_v = cos_ref[pl.ds(COARSE + MIDDLE, FINE), lanes]
            sin_v = sin_ref[pl.ds(COARSE + MIDDLE, FINE), lanes]
            fine_cos[pl.ds(u * FINE, FINE), :] = cos_u * cos_v - sin_u * sin_v
            fine_sin[pl.ds(u * FINE, FINE), :] = sin_u * cos_v + cos_u * sin_v
        for p in range(COARSE):
            cos_p, sin_p = cos_ref[pl.ds(p, 1), lanes], sin_ref[pl.ds(p, 1), lanes]
            table[pl.ds(p * 256, 256), :] = (cos_p * fine_cos[...] - sin_p * fine_sin[...]).astype(BF16)
        spectra = jnp.dot(filt[...], table[...], preferred_element_type=F32).astype(BF16)
        for core in range(2):
            group = to_z * 2 + core
            sent[group] = spectra[:, core * LANES : (core + 1) * LANES]

            @pl.when(group != me)
            def _():
                send(group).start()

        return carry

    lax.fori_loop(0, SHARDS // 2, transform, 0)

    def widen(shard, source):
        rows = pl.ds(pl.multiple_of(shard * FRAMES * INPUTS, FRAMES * INPUTS), FRAMES * INPUTS)
        spread[rows, :] = source.astype(F32)

    widen(me, sent[me])

    def arrive(i, carry):
        half = (i + 1) // 2
        shard = lax.rem(me + SHARDS + half * (1 - 2 * (i % 2)), SHARDS)
        pltpu.make_async_remote_copy(
            src_ref=sent.at[shard], dst_ref=landed.at[shard], send_sem=send_sems.at[shard],
            recv_sem=recv_sems.at[shard], device_id={"chan": shard}, device_id_type=MESH,
        ).wait_recv()
        widen(shard, landed[shard])
        return carry

    lax.fori_loop(1, SHARDS, arrive, 0)

    def turn(a, carry):
        block = spread[pl.ds(a, SPECTRA, stride=INPUTS), :].T
        turned_re[pl.ds(a, GROUP, stride=INPUTS), :] = block[:GROUP]
        turned_im[pl.ds(a, GROUP, stride=INPUTS), :] = block[GROUP:]
        return carry

    lax.fori_loop(0, INPUTS, turn, 0)

    def narrow(c, carry):
        rows = pl.ds(pl.multiple_of(c * INPUTS, INPUTS), INPUTS)
        out[c, :, pl.ds(0, SPECTRA)] = turned_re[rows, :].astype(BF16)
        out[c, :, pl.ds(SPECTRA, SPECTRA)] = turned_im[rows, :].astype(BF16)
        return carry

    lax.fori_loop(0, GROUP, narrow, 0)

    def drain(offset, carry):
        send(lax.rem(me + offset, SHARDS)).wait_send()
        return carry

    lax.fori_loop(1, SHARDS, drain, 0)


def turned_spectra(samples, taps, cos_table, sin_table):
    vmem = pl.BlockSpec(memory_space=pltpu.VMEM)
    rows = FRAMES * INPUTS
    return pl.pallas_call(
        spectra_kernel,
        out_shape=jax.ShapeDtypeStruct((GROUP, INPUTS, 2 * SPECTRA), BF16),
        in_specs=[pl.BlockSpec(memory_space=pl.ANY), vmem, vmem, vmem],
        out_specs=vmem,
        scratch_shapes=[
            pltpu.VMEM((INPUTS, HALO + FRAMES * FFT), BF16),
            pltpu.VMEM((rows, FFT), BF16),
            pltpu.VMEM((FFT, 2 * LANES), BF16),
            pltpu.VMEM((256, 2 * LANES), F32),
            pltpu.VMEM((256, 2 * LANES), F32),
            pltpu.VMEM((SHARDS, rows, LANES), BF16),
            pltpu.VMEM((SHARDS, rows, LANES), BF16),
            pltpu.VMEM((SPECTRA * INPUTS, LANES), F32),
            pltpu.VMEM((GROUP * INPUTS, SPECTRA), F32),
            pltpu.VMEM((GROUP * INPUTS, SPECTRA), F32),
            pltpu.SemaphoreType.DMA,
            pltpu.SemaphoreType.DMA((2,)),
            pltpu.SemaphoreType.DMA((SHARDS,)),
            pltpu.SemaphoreType.DMA((SHARDS,)),
        ],
        compiler_params=pltpu.CompilerParams(
            collective_id=0, has_side_effects=True, vmem_limit_bytes=VMEM_LIMIT
        ),
        name="spectra",
    )(samples, taps, cos_table, sin_table)


PAIR, UP, DOWN, FAR, PAIR_UP, PAIR_DOWN, PAIR_FAR, ROW = range(8)


def gather_kernel(own, columns, rows, local_sem, send_sems, recv_sems):
    blk = lax.axis_index("blk")
    grid = lax.axis_index("grid")
    y, x = blk // 2, blk % 2

    def at(y_to, x_to):
        return lax.rem(y_to, 4) * 2 + x_to

    pair = at(y, 1 - x)
    below, above, far = at(y + 3, x), at(y + 1, x), at(y + 2, x)
    pair_below, pair_above, pair_far = at(y + 3, 1 - x), at(y + 1, 1 - x), at(y + 2, 1 - x)
    across = {"blk": pair, "grid": 1 - grid}

    barrier = pltpu.get_barrier_semaphore()
    for partner in ({"blk": pair}, {"blk": below}, {"blk": above}, across):
        pl.semaphore_signal(barrier, inc=1, device_id=partner, device_id_type=MESH)
    pl.semaphore_wait(barrier, 4)

    def piece(i, count=1):
        return pl.ds(i * PIECE, PIECE * count)

    def copy(kind, i, source, slot, partner):
        target = rows.at[piece(i)] if kind == ROW else columns.at[slot, piece(i)]
        return pltpu.make_async_remote_copy(
            src_ref=source, dst_ref=target, send_sem=send_sems.at[kind], recv_sem=recv_sems.at[kind, i],
            device_id=partner, device_id_type=MESH,
        )

    def held(slot, i):
        return columns.at[slot, piece(i)]

    def arrived(kind, i):
        copy(kind, i, own.at[piece(i)], blk, {"blk": pair}).wait_recv()

    keep = pltpu.make_async_copy(own, columns.at[blk], local_sem)
    keep.start()

    def first(i, carry):
        mine = own.at[piece(i)]
        copy(PAIR, i, mine, blk, {"blk": pair}).start()
        copy(UP, i, mine, blk, {"blk": above}).start()
        copy(DOWN, i, mine, blk, {"blk": below}).start()
        return carry

    lax.fori_loop(0, PIECES, first, 0)

    def second(j, carry):
        i = 2 * j
        arrived(PAIR, i)
        copy(ROW, i, held(pair, i), pair, across).start()
        copy(PAIR_UP, i, held(pair, i), pair, {"blk": above}).start()
        copy(PAIR_DOWN, i, held(pair, i), pair, {"blk": below}).start()
        arrived(UP, i)
        copy(FAR, i, held(below, i), below, {"blk": above}).start()
        arrived(DOWN, i)
        k = i + 1
        arrived(UP, k)
        copy(PAIR_UP, k, held(below, k), below, {"blk": pair}).start()
        arrived(DOWN, k)
        copy(FAR, k, held(above, k), above, {"blk": below}).start()
        copy(PAIR_DOWN, k, held(above, k), above, {"blk": pair}).start()
        arrived(PAIR, k)
        copy(ROW, k, held(pair, k), pair, across).start()
        return carry

    lax.fori_loop(0, PIECES // 2, second, 0)

    def third(j, carry):
        i = 2 * j
        k = i + 1
        arrived(FAR, k)
        copy(PAIR_FAR, k, held(far, k), far, {"blk": pair}).start()
        arrived(FAR, i)
        arrived(PAIR_UP, i)
        arrived(PAIR_DOWN, i)

        @pl.when(j % 2 == 0)
        def _():
            copy(PAIR_FAR, i, held(pair_below, i), pair_below, {"blk": above}).start()

        @pl.when(j % 2 == 1)
        def _():
            copy(PAIR_FAR, i, held(pair_above, i), pair_above, {"blk": below}).start()

        return carry

    lax.fori_loop(0, PIECES // 2, third, 0)

    def fourth(j, carry):
        i = 2 * j
        k = i + 1
        arrived(PAIR_UP, k)
        arrived(PAIR_DOWN, k)
        arrived(PAIR_FAR, i)
        arrived(PAIR_FAR, k)
        arrived(ROW, i)
        arrived(ROW, k)
        return carry

    lax.fori_loop(0, PIECES // 2, fourth, 0)
    keep.wait()
    for kind in range(8):
        pltpu.make_async_remote_copy(
            src_ref=own, dst_ref=rows, send_sem=send_sems.at[kind], recv_sem=recv_sems.at[kind, 0],
            device_id={"blk": pair}, device_id_type=MESH,
        ).wait_send()


def gathered_spectra(own):
    anywhere = pl.BlockSpec(memory_space=pl.ANY)
    return pl.pallas_call(
        gather_kernel,
        out_shape=[
            jax.ShapeDtypeStruct((8,) + own.shape, BF16),
            jax.ShapeDtypeStruct(own.shape, BF16),
        ],
        in_specs=[anywhere],
        out_specs=[anywhere, anywhere],
        scratch_shapes=[
            pltpu.SemaphoreType.DMA,
            pltpu.SemaphoreType.DMA((8,)),
            pltpu.SemaphoreType.DMA((8, PIECES)),
        ],
        compiler_params=pltpu.CompilerParams(
            collective_id=1, has_side_effects=True, vmem_limit_bytes=VMEM_LIMIT
        ),
        name="gather",
    )(own)


CHANNELS = 8


def cross_kernel(first, second, columns, out):
    for c in range(CHANNELS):
        left = jnp.concatenate([first[c], second[c]], 0)
        quarter = jnp.concatenate([left[:, SPECTRA:], -left[:, :SPECTRA]], 1)
        right = columns[:, c].reshape(8 * INPUTS, 2 * SPECTRA)
        product = lax.dot_general(
            jnp.concatenate([left, quarter], 0), right, (((1,), (1,)), ((), ())), preferred_element_type=F32
        ) * (1.0 / SPECTRA)
        out[:, c] = product.reshape(2, 2, INPUTS, 8 * INPUTS)


def cross_products(first, second, columns):
    shape = (2, GROUP, 2, INPUTS, 8 * INPUTS)
    block = pl.BlockSpec((CHANNELS, INPUTS, 2 * SPECTRA), lambda i: (i, 0, 0))
    return pl.pallas_call(
        cross_kernel,
        grid=(GROUP // CHANNELS,),
        out_shape=jax.ShapeDtypeStruct(shape, F32),
        in_specs=[block, block, pl.BlockSpec((8, CHANNELS, INPUTS, 2 * SPECTRA), lambda i: (0, i, 0, 0))],
        out_specs=pl.BlockSpec((2, CHANNELS, 2, INPUTS, 8 * INPUTS), lambda i: (0, i, 0, 0, 0)),
        compiler_params=pltpu.CompilerParams(vmem_limit_bytes=VMEM_LIMIT),
        name="cross",
    )(first, second, columns)


def body(samples, pfb_taps, chan_select):
    cos_table, sin_table = phase_tables(chan_select)
    own = turned_spectra(samples[0], pfb_taps, cos_table, sin_table)
    columns, other = gathered_spectra(own)
    lower = lax.axis_index("grid") == 0
    return cross_products(jnp.where(lower, own, other), jnp.where(lower, other, own), columns)


def solution(mesh):
    return jax.shard_map(
        body,
        mesh=mesh,
        in_specs=(P("grid", "blk", "chan"), P(), P()),
        out_specs=P(None, "chan", None, "blk", "grid"),
        check_vma=False,
    )
```

time: 547 us -> 125 us (0.23)
  waiting for transfers between devices: 351 us -> 0 us
  Pallas kernels: 0 us -> 119 us
  other arithmetic: 66.7 us -> 3.8 us
  local copies, waits for them, and re-layouts: 58.1 us -> 2.53 us
  blocking collectives: 36 us -> 0 us
  matrix products: 15.2 us -> 0 us
  between operations: 13.5 us -> 0.04 us
    all_gather x1 -> x0, waiting for transfers between devices: 351 us -> none  [body(): gathered = lax.all_gather(turned, ('blk', 'grid'), axis=0, tiled=True)]
    pallas_call x0 -> x3, Pallas kernels: none -> 119 us  [the longest x1 62.6 us: gathered_spectra(): pl.pallas_call(gather_kernel, out_shape=[jax.ShapeDtypeStruct((8,) + own....]
    another operation x3 -> x0, other arithmetic: 46.1 us -> none
    all_to_all x1 -> x0, blocking collectives: 36 us -> none  [body(): lax.all_to_all(spectra, 'chan', split_axis=2, concat_axis=1, tiled=True)]
    transpose x2 -> x0, local copies, waits for them, and re-layouts: 27.8 us -> none  [the longest x1 24.3 us: cross_products(): right_side.transpose(3, 1, 2, 0)]
    dot_general x2 -> x0, matrix products: 15.2 us -> none  [the longest x1 8.8 us: cross_products(): jnp.einsum('cak,ckb->cab', left_side, right_side, preferred_element_type=...]
    transpose x1 -> x0, other arithmetic: 14 us -> none  [cross_products(): right_side.transpose(3, 1, 2, 0)]
    dynamic_slice x2 -> x0, local copies, waits for them, and re-layouts: 12.5 us -> none  [the longest x1 10.8 us: body(): lax.dynamic_index_in_dim(gathered, lax.axis_index('grid'), 1, False)]
  transfers between devices with their start and end apart: 2 -> 0, of which waited for: 1 -> 0; matrix products, arithmetic and copies ran while one was open for 8% -> 0% of each run, Pallas kernels for 0% -> 0%
where the time goes in v1:
time: 125 us
  Pallas kernels  119 us (95%)
  other arithmetic  3.8 us (3%)
  local copies, waits for them, and re-layouts  2.53 us (2%)
    pallas_call x1, Pallas kernels, gathered_spectra(): pl.pallas_call(gather_kernel, out_shape=[jax.ShapeDtypeStruct((8,) + own....  62.6 us
    pallas_call x1, Pallas kernels, turned_spectra(): pl.pallas_call(spectra_kernel, out_shape=jax.ShapeDtypeStruct((GROUP, INP...  45.2 us
    pallas_call x1, Pallas kernels, cross_products(): pl.pallas_call(cross_kernel, grid=(GROUP // CHANNELS,), out_shape=jax.Sha...  10.9 us

profile of v1, /device:TPU:1, one launch (start us, length us, event | category | flops | bytes accessed | tf_op | source)
XLA Modules:
  0.0 125.0 jit_solution(17278784185951133026)
XLA Ops:
  0.0 0.8 broadcast_in_dim.27
  0.8 0.1 mul.54
  0.9 1.4 %fusion.3 = (f32[40,2048]{1,0:T(8,128)S(1)}, f32[40,2048]{1,0:T(8,128)S(1)}) fusion(s32[2048]{0:T(1024)S(1)} %fusion.6, s32[2048]{0:T(1024)S(1)} %mul.54, s32[40]{0:T(128)S(1)} %compare_select_fusion, pred[40]{0:T(512)(128)(4,1)S(1)} %iota_compare_fusion), kind=kLoop, calls=%fused_computation.8 | loop fusion | flops 1310720 | bytes 671944 | tf_op jit(solution)/shard_map/sin | solution.py:38
  2.3 0.0 copy-start.1
  2.3 0.7 copy-done.1
  3.0 45.2 %spectra.1.own = bf16[64,32,256]{2,1,0:T(8,128)(2,1)S(1)} custom-call(bf16[32,16384]{1,0:T(8,128)(2,1)} %bitcast.1, bf16[4,2048]{1,0:T(4,128)(2,1)S(1)} %copy-done.1, f32[40,2048]{1,0:T(8,128)S(1)} %get-tuple-element.12.cos_ref, f32[40,2048]{1,0:T(8,128)S(1)} %get-tuple-element.11.sin_ref), custom_call_target="tpu_custom_call" | custom-call | tf_op jit(solution)/shard_map/spectra/pallas_call | solution.py:178
  48.2 0.0 copy-start
  48.2 1.0 copy-done
  49.1 62.6 %gather.1 = (bf16[8,64,32,256]{3,2,1,0:T(8,128)(2,1)}, bf16[64,32,256]{2,1,0:T(8,128)(2,1)S(1)}) custom-call(bf16[64,32,256]{2,1,0:T(8,128)(2,1)} %copy-done), custom_call_target="tpu_custom_call" | custom-call | tf_op jit(solution)/shard_map/gather/pallas_call | solution.py:319
  111.8 2.4 %broadcast_select_fusion = (bf16[64,32,256]{2,1,0:T(8,128)(2,1)}, bf16[64,32,256]{2,1,0:T(8,128)(2,1)S(1)}) fusion(bf16[64,32,256]{2,1,0:T(8,128)(2,1)S(1)} %get-tuple-element.7, bf16[64,32,256]{2,1,0:T(8,128)(2,1)} %copy-done, pred[]{:T(512)S(6)} %eq.7), kind=kLoop, calls=%fused_computation | loop fusion | flops 1048576 | bytes 4194305 | tf_op jit(solution)/shard_map/jit(_where)/select_n | solution.py:372
  114.2 10.9 %cross.1 = f32[2,64,2,32,256]{4,3,2,1,0:T(8,128)} custom-call(bf16[64,32,256]{2,1,0:T(8,128)(2,1)S(1)} %get-tuple-element.10.first, bf16[64,32,256]{2,1,0:T(8,128)(2,1)} %get-tuple-element.9.second, bf16[8,64,32,256]{3,2,1,0:T(8,128)(2,1)} %get-tuple-element.8.columns), custom_call_target="tpu_custom_call" | custom-call | tf_op jit(solution)/shard_map/cross/pallas_call | solution.py:356
  (4 shorter events, 0.0 us)
Async XLA Ops:
  2.3 0.7 copy-start.1
  48.2 1.0 copy-start

commit v2 on v0

v2 whole, which is shorter than its diff:
```python
import math

import jax
import jax.numpy as jnp
from jax import lax
from jax.experimental import pallas as pl
from jax.experimental.pallas import tpu as pltpu
from jax.sharding import PartitionSpec as P

MESH = pl.DeviceIdType.MESH
BF16 = jnp.bfloat16
F32 = jnp.float32
VMEM_LIMIT = 22 * 1024 * 1024
CROSS_LIMIT = 24 * 1024 * 1024

FFT = 2048
TAPS = 4
INPUTS = 32
FRAMES = 8
GROUP = 64
SHARDS = 16
SPECTRA = SHARDS * FRAMES
LANES = 2 * GROUP
HALO = (TAPS - 1) * FFT
COARSE, MIDDLE, FINE = 8, 16, 16

PARTS = 4
STEPS = FRAMES // 2
PART = INPUTS // 2
HEIGHT = STEPS * PART
DEPTH = SHARDS * STEPS
BLOCK = (PARTS, GROUP, PART, 2 * DEPTH)
PIECES = ((0, 18), (18, 18), (36, 14), (50, 14))
PAIR, UP, DOWN, FAR, PAIR_UP, PAIR_DOWN, PAIR_FAR, ROW = range(8)


def cos_sin(phase):
    turns = (phase + FFT // 8) // (FFT // 4)
    angle = (phase - turns * (FFT // 4)).astype(F32) * (2.0 * math.pi / FFT)
    square = angle * angle
    cosine = 1.0 + square * (-1.0 / 2 + square * (1.0 / 24 + square * (-1.0 / 720 + square * (1.0 / 40320))))
    sine = angle * (1.0 + square * (-1.0 / 6 + square * (1.0 / 120 + square * (-1.0 / 5040 + square * (1.0 / 362880)))))
    odd = turns % 2 == 1
    out_cos = jnp.where(odd, sine, cosine)
    out_sin = jnp.where(odd, cosine, sine)
    return (
        jnp.where((turns == 1) | (turns == 2), -out_cos, out_cos),
        jnp.where((turns == 2) | (turns == 3), -out_sin, out_sin),
    )


def spectra_kernel(
    samples, taps, chan_select, columns, rows, history, filt, table, fine_cos, fine_sin, sent, landed,
    spread, turned, own, halo_sems, turn_send, turn_recv, keep_sems, send_sems, recv_sems,
):
    me = lax.axis_index("chan")
    blk = lax.axis_index("blk")
    grid = lax.axis_index("grid")
    my_z = me // 2
    y, x = blk // 2, blk % 2

    def at(y_to, x_to):
        return lax.rem(y_to, 4) * 2 + x_to

    pair = at(y, 1 - x)
    below, above, far = at(y + 3, x), at(y + 1, x), at(y + 2, x)
    pair_below, pair_above = at(y + 3, 1 - x), at(y + 1, 1 - x)
    to_pair, to_below, to_above = {"blk": pair}, {"blk": below}, {"blk": above}
    to_across = {"blk": pair, "grid": 1 - grid}

    barrier = pltpu.get_barrier_semaphore()

    def greet(offset, carry):
        pl.semaphore_signal(barrier, inc=1, device_id={"chan": lax.rem(me + offset, SHARDS)}, device_id_type=MESH)
        return carry

    lax.fori_loop(1, SHARDS, greet, 0)
    for partner in (to_pair, to_below, to_above, to_across):
        pl.semaphore_signal(barrier, inc=1, device_id=partner, device_id_type=MESH)

    width = 512

    def filter_frames(early):
        for step in range(STEPS):
            s = step + STEPS * (1 - early)

            def part(i, carry):
                lanes = pl.multiple_of(i * width, width)
                total = jnp.zeros((INPUTS, width), F32)
                for t in range(TAPS):
                    weight = taps[pl.ds(t, 1), pl.ds(lanes, width)].astype(F32)
                    frame = s + t - (TAPS - 1)
                    if frame < 0:
                        source = history[:, pl.ds((s + t) * FFT + lanes, width)]
                    else:
                        source = samples[:, pl.ds(frame * FFT + lanes, width)]
                    total = total + weight * source.astype(F32)
                total = total.astype(BF16)
                for half in range(2):
                    place = pl.ds(((2 * early + half) * STEPS + step) * PART, PART)
                    filt[place, pl.ds(lanes, width)] = total[half * PART : (half + 1) * PART]
                return carry

            lax.fori_loop(0, FFT // width, part, 0)

    filter_frames(0)
    pl.semaphore_wait(barrier, SHARDS - 1 + 4)

    def send(part, group):
        return pltpu.make_async_remote_copy(
            src_ref=sent.at[part, group],
            dst_ref=landed.at[part, me],
            send_sem=turn_send.at[part, group],
            recv_sem=turn_recv.at[part, me],
            device_id={"chan": group},
            device_id_type=MESH,
        )

    def chip(i):
        away = 4 + (i + 1) // 2 * (1 - 2 * (i % 2))
        return lax.rem(my_z + away, SHARDS // 2)

    def leave(part, group):
        @pl.when(group != me)
        def _():
            send(part, group).start()

    def leave_later(part):
        def step(i, carry):
            for core in range(2):
                leave(part, chip(i) * 2 + core)
            return carry

        lax.fori_loop(0, SHARDS // 2, step, 0)

    def build_table(to_z):
        bins = jnp.broadcast_to(chan_select[pl.ds(to_z, 1), :], (8, LANES))
        other = pltpu.roll(bins, GROUP, 1)
        low = lax.broadcasted_iota(jnp.int32, (8, LANES), 1) < GROUP
        bins = jnp.concatenate([jnp.where(low, bins, other), jnp.where(low, other, bins)], 1)
        quarter = jnp.where(low, 0, FFT // 4)
        quarter = jnp.concatenate([quarter, quarter], 1)
        row = lax.broadcasted_iota(jnp.int32, (8, 2 * LANES), 0)
        cos_p, sin_p = cos_sin(row * 256 * bins % FFT)
        middle = [cos_sin((row + 8 * k) * 16 * bins % FFT) for k in range(MIDDLE // 8)]
        fine = [cos_sin(((row + 8 * k) * bins + quarter) % FFT) for k in range(FINE // 8)]
        cos_v = jnp.concatenate([both[0] for both in fine], 0)
        sin_v = jnp.concatenate([both[1] for both in fine], 0)
        for u in range(MIDDLE):
            cos_u, sin_u = (t[u % 8 : u % 8 + 1] for t in middle[u // 8])
            fine_cos[pl.ds(u * FINE, FINE), :] = cos_u * cos_v - sin_u * sin_v
            fine_sin[pl.ds(u * FINE, FINE), :] = sin_u * cos_v + cos_u * sin_v
        for p in range(COARSE):
            place = pl.ds(p * 256, 256)
            turned_on = cos_p[p : p + 1] * fine_cos[...] - sin_p[p : p + 1] * fine_sin[...]
            table[to_z, place, :] = turned_on.astype(BF16)

    def transform(early, to_z):
        spectra = jnp.dot(filt[pl.ds(early * 2 * HEIGHT, 2 * HEIGHT), :], table[to_z], preferred_element_type=F32)
        spectra = spectra.astype(BF16)
        for core in range(2):
            for half in range(2):
                sent[2 * early + half, to_z * 2 + core] = spectra[
                    half * HEIGHT : (half + 1) * HEIGHT, core * LANES : (core + 1) * LANES
                ]

    def later_frames(i, carry):
        to_z = chip(i)
        build_table(to_z)
        transform(0, to_z)
        for core in range(2):
            leave(0, to_z * 2 + core)
        return carry

    lax.fori_loop(0, SHARDS // 2, later_frames, 0)

    halo = pltpu.make_async_remote_copy(
        src_ref=samples.at[:, pl.ds((FRAMES - TAPS + 1) * FFT, HALO)],
        dst_ref=history,
        send_sem=halo_sems.at[0],
        recv_sem=halo_sems.at[1],
        device_id={"chan": lax.rem(me + 1, SHARDS)},
        device_id_type=MESH,
    )
    halo.start()
    leave_later(1)

    def early_frames():
        halo.wait_send()
        halo.wait_recv()

        @pl.when(me == 0)
        def _():
            history[...] = jnp.zeros((INPUTS, HALO), BF16)

        filter_frames(1)

        def step(i, carry):
            to_z = chip(i)
            transform(1, to_z)
            for core in range(2):
                leave(2, to_z * 2 + core)
            return carry

        lax.fori_loop(0, SHARDS // 2, step, 0)
        leave_later(3)

    def widen(shard, source):
        spread[pl.ds(pl.multiple_of(shard * HEIGHT, HEIGHT), HEIGHT), :] = source.astype(F32)

    def turn_part(part):
        widen(me, sent[part, me])

        def arrive(i, carry):
            shard = lax.rem(me + SHARDS + (i + 1) // 2 * (1 - 2 * (i % 2)), SHARDS)
            pltpu.make_async_remote_copy(
                src_ref=sent.at[part, shard], dst_ref=landed.at[part, shard], send_sem=turn_send.at[part, shard],
                recv_sem=turn_recv.at[part, shard], device_id={"chan": shard}, device_id_type=MESH,
            ).wait_recv()
            widen(shard, landed[part, shard])
            return carry

        lax.fori_loop(1, SHARDS, arrive, 0)
        low = lax.broadcasted_iota(jnp.int32, (GROUP, 2 * DEPTH), 1) < DEPTH

        def turn(k, carry):
            for j in range(2):
                a = 4 * k + 2 * j
                both = jnp.concatenate([spread[pl.ds(a + b, DEPTH, stride=PART), :] for b in range(2)], 0).T
                real, imag = both[:GROUP], both[GROUP:]
                turned[pl.ds(a, GROUP, stride=PART), :] = jnp.where(low, real, pltpu.roll(imag, DEPTH, 1))
                turned[pl.ds(a + 1, GROUP, stride=PART), :] = jnp.where(low, pltpu.roll(real, DEPTH, 1), imag)
            return carry

        lax.fori_loop(0, PART // 4, turn, 0)

        def narrow(c, carry):
            place = pl.ds(pl.multiple_of(c * 8 * PART, 8 * PART), 8 * PART)
            own[part, pl.ds(c * 8, 8)] = turned[place, :].astype(BF16).reshape(8, PART, 2 * DEPTH)
            return carry

        lax.fori_loop(0, GROUP // 8, narrow, 0)

    def copy(kind, part, i, partner):
        channels = pl.ds(*PIECES[i])
        return pltpu.make_async_remote_copy(
            src_ref=own.at[part, channels], dst_ref=columns.at[blk, part, channels],
            send_sem=send_sems.at[kind, part], recv_sem=recv_sems.at[kind, part, i],
            device_id=partner, device_id_type=MESH,
        )

    def arrived(kind, part, i):
        copy(kind, part, i, to_pair).wait_recv()

    def keep(part):
        return [
            pltpu.make_async_copy(own.at[part], columns.at[blk, part], keep_sems.at[0, part]),
            pltpu.make_async_copy(own.at[part], rows.at[grid, part], keep_sems.at[1, part]),
        ]

    def first(part):
        for i in (0, 2, 1, 3):
            copy(PAIR, part, i, to_pair).start()
            copy(UP, part, i, to_above).start()
            copy(DOWN, part, i, to_below).start()
        for local in keep(part):
            local.start()

    def pass_on(kind, part, i, slot, partner):
        channels = pl.ds(*PIECES[i])
        target = rows.at[grid, part, channels] if kind == ROW else columns.at[slot, part, channels]
        pltpu.make_async_remote_copy(
            src_ref=columns.at[slot, part, channels], dst_ref=target,
            send_sem=send_sems.at[kind, part], recv_sem=recv_sems.at[kind, part, i],
            device_id=partner, device_id_type=MESH,
        ).start()

    def pass_far(part, i):
        if i % 2 == 0:
            pass_on(FAR, part, i, below, to_above)
        else:
            pass_on(FAR, part, i, above, to_below)

    def second(part):
        for i in (0, 2, 1, 3):
            arrived(PAIR, part, i)
            arrived(UP, part, i)
            arrived(DOWN, part, i)
            if i < 2:
                pass_on(PAIR_UP, part, i, pair, to_above)
                pass_on(PAIR_DOWN, part, i, pair, to_below)
            else:
                pass_on(PAIR_UP, part, i, below, to_pair)
                pass_on(PAIR_DOWN, part, i, above, to_pair)
            pass_far(part, i)
            pass_on(ROW, part, i, pair, to_across)

    def third(part):
        for i in (2, 0, 3, 1):
            arrived(FAR, part, i)
            if i >= 2:
                pass_on(PAIR_FAR, part, i, far, to_pair)
            else:
                arrived(PAIR_UP, part, i)
                arrived(PAIR_DOWN, part, i)
                if i == 0:
                    pass_on(PAIR_FAR, part, i, pair_below, to_above)
                else:
                    pass_on(PAIR_FAR, part, i, pair_above, to_below)

    def fourth(part):
        for i in (2, 3):
            arrived(PAIR_UP, part, i)
            arrived(PAIR_DOWN, part, i)
        for i in range(4):
            arrived(PAIR_FAR, part, i)
            arrived(ROW, part, i)

    turn_part(0)
    first(0)
    early_frames()
    turn_part(1)
    first(1)
    second(0)
    turn_part(2)
    first(2)
    second(1)
    third(0)
    turn_part(3)
    first(3)
    second(2)
    third(1)
    second(3)
    third(2)
    third(3)
    for part in range(PARTS):
        fourth(part)
    for part in range(PARTS):
        for local in keep(part):
            local.wait()
        for kind in range(8):
            pltpu.make_async_remote_copy(
                src_ref=own.at[part], dst_ref=columns.at[0, part], send_sem=send_sems.at[kind, part],
                recv_sem=recv_sems.at[kind, part, 0], device_id=to_pair, device_id_type=MESH,
            ).wait_send()

    def drain(offset, carry):
        for part in range(PARTS):
            send(part, lax.rem(me + offset, SHARDS)).wait_send()
        return carry

    lax.fori_loop(1, SHARDS, drain, 0)


def gathered_spectra(samples, taps, chan_select):
    vmem = pl.BlockSpec(memory_space=pltpu.VMEM)
    anywhere = pl.BlockSpec(memory_space=pl.ANY)
    return pl.pallas_call(
        spectra_kernel,
        out_shape=[
            jax.ShapeDtypeStruct((8,) + BLOCK, BF16),
            jax.ShapeDtypeStruct((2,) + BLOCK, BF16),
        ],
        in_specs=[vmem, vmem, vmem],
        out_specs=[anywhere, anywhere],
        scratch_shapes=[
            pltpu.VMEM((INPUTS, HALO), BF16),
            pltpu.VMEM((PARTS * HEIGHT, FFT), BF16),
            pltpu.VMEM((SHARDS // 2, FFT, 2 * LANES), BF16),
            pltpu.VMEM((256, 2 * LANES), F32),
            pltpu.VMEM((256, 2 * LANES), F32),
            pltpu.VMEM((PARTS, SHARDS, HEIGHT, LANES), BF16),
            pltpu.VMEM((PARTS, SHARDS, HEIGHT, LANES), BF16),
            pltpu.VMEM((SHARDS * HEIGHT, LANES), F32),
            pltpu.VMEM((GROUP * PART, 2 * DEPTH), F32),
            pltpu.VMEM(BLOCK, BF16),
            pltpu.SemaphoreType.DMA((2,)),
            pltpu.SemaphoreType.DMA((PARTS, SHARDS)),
            pltpu.SemaphoreType.DMA((PARTS, SHARDS)),
            pltpu.SemaphoreType.DMA((2, PARTS)),
            pltpu.SemaphoreType.DMA((8, PARTS)),
            pltpu.SemaphoreType.DMA((8, PARTS, len(PIECES))),
        ],
        compiler_params=pltpu.CompilerParams(
            collective_id=0, has_side_effects=True, vmem_limit_bytes=VMEM_LIMIT
        ),
        name="spectra",
    )(samples, taps, chan_select)


CHANNELS = 8
CHUNKS = GROUP // CHANNELS


def cross_kernel(rows, columns, out, products, out_sems):
    sign = jnp.where(lax.broadcasted_iota(jnp.int32, (2 * INPUTS, 2 * DEPTH), 1) < DEPTH, 1.0, -1.0).astype(BF16)

    def store(i):
        channels = pl.ds(i * CHANNELS, CHANNELS)
        return pltpu.make_async_copy(products.at[:, channels], out.at[:, channels], out_sems.at[i])

    def operand(data, c):
        early_and_late = []
        for early in range(2):
            halves = [data[:, 2 * early + half, c] for half in range(2)]
            early_and_late.append(jnp.stack(halves, 1).reshape(-1, 2 * DEPTH))
        return early_and_late

    def multiply(i, carry):
        for j in range(CHANNELS):
            c = i * CHANNELS + j
            left = operand(rows, c)
            quarter = [jnp.concatenate([block[:, DEPTH:], block[:, :DEPTH]], 1) * sign for block in left]
            left = jnp.concatenate([jnp.concatenate(left, 1), jnp.concatenate(quarter, 1)], 0)
            product = lax.dot_general(
                left, jnp.concatenate(operand(columns, c), 1), (((1,), (1,)), ((), ())),
                preferred_element_type=F32,
            ) * (1.0 / SPECTRA)
            products[:, c] = product.reshape(2, 2, INPUTS, 8 * INPUTS)
        store(i).start()
        return carry

    lax.fori_loop(0, CHUNKS, multiply, 0)

    def finish(i, carry):
        store(i).wait()
        return carry

    lax.fori_loop(0, CHUNKS, finish, 0)


def cross_products(rows, columns):
    shape = (2, GROUP, 2, INPUTS, 8 * INPUTS)
    return pl.pallas_call(
        cross_kernel,
        out_shape=jax.ShapeDtypeStruct(shape, F32),
        in_specs=[pl.BlockSpec(memory_space=pltpu.VMEM)] * 2,
        out_specs=pl.BlockSpec(memory_space=pltpu.HBM),
        scratch_shapes=[pltpu.VMEM(shape, F32), pltpu.SemaphoreType.DMA((CHUNKS,))],
        compiler_params=pltpu.CompilerParams(vmem_limit_bytes=CROSS_LIMIT),
        name="cross",
    )(rows, columns)


def body(samples, pfb_taps, chan_select):
    columns, rows = gathered_spectra(samples[0], pfb_taps, chan_select.reshape(SHARDS // 2, LANES))
    return cross_products(rows, columns)


def solution(mesh):
    return jax.shard_map(
        body,
        mesh=mesh,
        in_specs=(P("grid", "blk", "chan"), P(), P()),
        out_specs=P(None, "chan", None, "blk", "grid"),
        check_vma=False,
    )
```

time: 547 us -> 89.1 us (0.16)
  waiting for transfers between devices: 351 us -> 0 us
  Pallas kernels: 0 us -> 84.8 us
  other arithmetic: 66.7 us -> 0 us
  local copies, waits for them, and re-layouts: 58.1 us -> 2.63 us
  blocking collectives: 36 us -> 0 us
  matrix products: 15.2 us -> 0 us
  between operations: 13.5 us -> 0.01 us
    all_gather x1 -> x0, waiting for transfers between devices: 351 us -> none  [body(): gathered = lax.all_gather(turned, ('blk', 'grid'), axis=0, tiled=True)]
    pallas_call x0 -> x2, Pallas kernels: none -> 84.8 us  [the longest x1 79.9 us: gathered_spectra(): pl.pallas_call(spectra_kernel, out_shape=[jax.ShapeDtypeStruct((8,) + BLO...]
    another operation x3 -> x0, other arithmetic: 46.1 us -> none
    all_to_all x1 -> x0, blocking collectives: 36 us -> none  [body(): lax.all_to_all(spectra, 'chan', split_axis=2, concat_axis=1, tiled=True)]
    transpose x2 -> x0, local copies, waits for them, and re-layouts: 27.8 us -> none  [the longest x1 24.3 us: cross_products(): right_side.transpose(3, 1, 2, 0)]
    dot_general x2 -> x0, matrix products: 15.2 us -> none  [the longest x1 8.8 us: cross_products(): jnp.einsum('cak,ckb->cab', left_side, right_side, preferred_element_type=...]
    transpose x1 -> x0, other arithmetic: 14 us -> none  [cross_products(): right_side.transpose(3, 1, 2, 0)]
    dynamic_slice x2 -> x0, local copies, waits for them, and re-layouts: 12.5 us -> none  [the longest x1 10.8 us: body(): lax.dynamic_index_in_dim(gathered, lax.axis_index('grid'), 1, False)]
  transfers between devices with their start and end apart: 2 -> 0, of which waited for: 1 -> 0; matrix products, arithmetic and copies ran while one was open for 8% -> 0% of each run, Pallas kernels for 0% -> 0%
where the time goes in v2:
time: 89.1 us; the launch traced here: 87.4 us
  Pallas kernels  84.8 us (95%)
  local copies, waits for them, and re-layouts  2.63 us (3%)
    pallas_call x1, Pallas kernels, gathered_spectra(): pl.pallas_call(spectra_kernel, out_shape=[jax.ShapeDtypeStruct((8,) + BLO...  79.9 us
    pallas_call x1, Pallas kernels, cross_products(): pl.pallas_call(cross_kernel, out_shape=jax.ShapeDtypeStruct(shape, F32),...  4.88 us
    unnamed x6, local copies, waits for them, and re-layouts  2.63 us

profile of v2, /device:TPU:1, one launch (start us, length us, event | category | flops | bytes accessed | tf_op | source)
XLA Modules:
  0.0 87.4 jit_solution(2119724790313072500)
XLA Ops:
  0.0 0.0 copy-start
  0.0 1.2 %copy-done = bf16[1,32,16384]{2,1,0:T(8,128)(2,1)S(1)} copy-done((bf16[1,32,16384]{2,1,0:T(8,128)(2,1)S(1)}, bf16[1,32,16384]{2,1,0:T(8,128)(2,1)}, u32[]{:S(2)}) %copy-start) | copy-done | bytes 1048600
  1.2 0.0 copy-start.1
  1.2 0.7 copy-done.1
  1.9 0.0 copy-start.2
  1.9 0.7 copy-done.2
  2.6 79.9 %spectra.1 = (bf16[8,4,64,16,128]{4,3,2,1,0:T(8,128)(2,1)S(1)}, bf16[2,4,64,16,128]{4,3,2,1,0:T(8,128)(2,1)S(1)}) custom-call(bf16[32,16384]{1,0:T(8,128)(2,1)S(1)} %bitcast.2, bf16[4,2048]{1,0:T(4,128)(2,1)S(1)} %copy-done.1, s32[8,128]{1,0:T(8,128)S(1)} %bitcast.3), custom_call_target="tpu_custom_call" | custom-call | tf_op jit(solution)/shard_map/spectra/pallas_call | solution.py:358
  82.5 4.9 %cross.1 = f32[2,64,2,32,256]{4,3,2,1,0:T(8,128)} custom-call(bf16[2,4,64,16,128]{4,3,2,1,0:T(8,128)(2,1)S(1)} %get-tuple-element.7.rows, bf16[8,4,64,16,128]{4,3,2,1,0:T(8,128)(2,1)S(1)} %get-tuple-element.8.columns), custom_call_target="tpu_custom_call" | custom-call | tf_op jit(solution)/shard_map/cross/pallas_call | solution.py:434
Async XLA Ops:
  0.0 1.2 %copy-start = (bf16[1,32,16384]{2,1,0:T(8,128)(2,1)S(1)}, bf16[1,32,16384]{2,1,0:T(8,128)(2,1)}, u32[]{:S(2)}) copy-start(bf16[1,32,16384]{2,1,0:T(8,128)(2,1)} %param.3) | copy-start | bytes 3145732
  1.2 0.7 copy-start.1
  1.9 0.7 copy-start.2

commit v3 on v2

--- a/solution.py
+++ b/solution.py
@@ -30,7 +30,7 @@
 HEIGHT = STEPS * PART
 DEPTH = SHARDS * STEPS
 BLOCK = (PARTS, GROUP, PART, 2 * DEPTH)
-PIECES = ((0, 18), (18, 18), (36, 14), (50, 14))
+SPLIT = 36
 PAIR, UP, DOWN, FAR, PAIR_UP, PAIR_DOWN, PAIR_FAR, ROW = range(8)
 
 
@@ -50,8 +50,8 @@
 
 
 def spectra_kernel(
-    samples, taps, chan_select, columns, rows, history, filt, table, fine_cos, fine_sin, sent, landed,
-    spread, turned, own, halo_sems, turn_send, turn_recv, keep_sems, send_sems, recv_sems,
+    samples, taps, chan_select, columns, rows, history, filt, fine_cos, fine_sin, sent, landed,
+    spread, turned, own, halo_sems, turn_send, turn_recv, keep_sems, send_sems, recv_sems, *tables,
 ):
     me = lax.axis_index("chan")
     blk = lax.axis_index("blk")
@@ -107,33 +107,36 @@
     pl.semaphore_wait(barrier, SHARDS - 1 + 4)
 
     def send(part, group):
-        return pltpu.make_async_remote_copy(
+        pltpu.make_async_remote_copy(
             src_ref=sent.at[part, group],
             dst_ref=landed.at[part, me],
-            send_sem=turn_send.at[part, group],
-            recv_sem=turn_recv.at[part, me],
+            send_sem=turn_send.at[part],
+            recv_sem=turn_recv.at[part],
             device_id={"chan": group},
             device_id_type=MESH,
+        ).start()
+
+    def all_sent(part):
+        return pltpu.make_async_remote_copy(
+            src_ref=sent.at[part, pl.ds(0, SHARDS - 1)],
+            dst_ref=landed.at[part, pl.ds(0, SHARDS - 1)],
+            send_sem=turn_send.at[part],
+            recv_sem=turn_recv.at[part],
+            device_id={"chan": lax.rem(me + 1, SHARDS)},
+            device_id_type=MESH,
         )
 
-    def chip(i):
-        away = 4 + (i + 1) // 2 * (1 - 2 * (i % 2))
-        return lax.rem(my_z + away, SHARDS // 2)
-
-    def leave(part, group):
-        @pl.when(group != me)
-        def _():
-            send(part, group).start()
-
-    def leave_later(part):
-        def step(i, carry):
+    chips = [lax.rem(my_z + away, SHARDS // 2) for away in (4, 3, 5, 2, 6, 1, 7, 0)]
+
+    def leave(part, i):
+        if i < len(chips) - 1:
             for core in range(2):
-                leave(part, chip(i) * 2 + core)
-            return carry
-
-        lax.fori_loop(0, SHARDS // 2, step, 0)
-
-    def build_table(to_z):
+                send(part, chips[i] * 2 + core)
+        else:
+            send(part, my_z * 2 + 1 - me % 2)
+
+    def build_table(i):
+        to_z, table = chips[i], tables[i]
         bins = jnp.broadcast_to(chan_select[pl.ds(to_z, 1), :], (8, LANES))
         other = pltpu.roll(bins, GROUP, 1)
         low = lax.broadcasted_iota(jnp.int32, (8, LANES), 1) < GROUP
@@ -153,10 +156,11 @@
         for p in range(COARSE):
             place = pl.ds(p * 256, 256)
             turned_on = cos_p[p : p + 1] * fine_cos[...] - sin_p[p : p + 1] * fine_sin[...]
-            table[to_z, place, :] = turned_on.astype(BF16)
-
-    def transform(early, to_z):
-        spectra = jnp.dot(filt[pl.ds(early * 2 * HEIGHT, 2 * HEIGHT), :], table[to_z], preferred_element_type=F32)
+            table[place, :] = turned_on.astype(BF16)
+
+    def transform(early, i):
+        to_z = chips[i]
+        spectra = jnp.dot(filt[pl.ds(early * 2 * HEIGHT, 2 * HEIGHT), :], tables[i][...], preferred_element_type=F32)
         spectra = spectra.astype(BF16)
         for core in range(2):
             for half in range(2):
@@ -164,15 +168,12 @@
                     half * HEIGHT : (half + 1) * HEIGHT, core * LANES : (core + 1) * LANES
                 ]
 
-    def later_frames(i, carry):
-        to_z = chip(i)
-        build_table(to_z)
-        transform(0, to_z)
-        for core in range(2):
-            leave(0, to_z * 2 + core)
-        return carry
-
-    lax.fori_loop(0, SHARDS // 2, later_frames, 0)
+    build_table(0)
+    for i in range(len(chips)):
+        if i + 1 < len(chips):
+            build_table(i + 1)
+        transform(0, i)
+        leave(0, i)
 
     halo = pltpu.make_async_remote_copy(
         src_ref=samples.at[:, pl.ds((FRAMES - TAPS + 1) * FFT, HALO)],
@@ -183,7 +184,8 @@
         device_id_type=MESH,
     )
     halo.start()
-    leave_later(1)
+    for i in range(len(chips)):
+        leave(1, i)
 
     def early_frames():
         halo.wait_send()
@@ -194,33 +196,22 @@
             history[...] = jnp.zeros((INPUTS, HALO), BF16)
 
         filter_frames(1)
-
-        def step(i, carry):
-            to_z = chip(i)
-            transform(1, to_z)
-            for core in range(2):
-                leave(2, to_z * 2 + core)
+        for i in range(len(chips)):
+            transform(1, i)
+            leave(2, i)
+        for i in range(len(chips)):
+            leave(3, i)
+
+    def turn_part(part):
+        landed[part, me] = sent[part, me]
+        all_sent(part).wait_recv()
+
+        def widen(i, carry):
+            place = pl.ds(pl.multiple_of(i * 4 * HEIGHT, 4 * HEIGHT), 4 * HEIGHT)
+            spread[place, :] = landed[part, pl.ds(i * 4, 4)].astype(F32).reshape(4 * HEIGHT, LANES)
             return carry
 
-        lax.fori_loop(0, SHARDS // 2, step, 0)
-        leave_later(3)
-
-    def widen(shard, source):
-        spread[pl.ds(pl.multiple_of(shard * HEIGHT, HEIGHT), HEIGHT), :] = source.astype(F32)
-
-    def turn_part(part):
-        widen(me, sent[part, me])
-
-        def arrive(i, carry):
-            shard = lax.rem(me + SHARDS + (i + 1) // 2 * (1 - 2 * (i % 2)), SHARDS)
-            pltpu.make_async_remote_copy(
-                src_ref=sent.at[part, shard], dst_ref=landed.at[part, shard], send_sem=turn_send.at[part, shard],
-                recv_sem=turn_recv.at[part, shard], device_id={"chan": shard}, device_id_type=MESH,
-            ).wait_recv()
-            widen(shard, landed[part, shard])
-            return carry
-
-        lax.fori_loop(1, SHARDS, arrive, 0)
+        lax.fori_loop(0, SHARDS // 4, widen, 0)
         low = lax.broadcasted_iota(jnp.int32, (GROUP, 2 * DEPTH), 1) < DEPTH
 
         def turn(k, carry):
@@ -235,86 +226,53 @@
         lax.fori_loop(0, PART // 4, turn, 0)
 
         def narrow(c, carry):
-            place = pl.ds(pl.multiple_of(c * 8 * PART, 8 * PART), 8 * PART)
-            own[part, pl.ds(c * 8, 8)] = turned[place, :].astype(BF16).reshape(8, PART, 2 * DEPTH)
+            place = pl.ds(pl.multiple_of(c * 16 * PART, 16 * PART), 16 * PART)
+            own[part, pl.ds(c * 16, 16)] = turned[place, :].astype(BF16).reshape(16, PART, 2 * DEPTH)
             return carry
 
-        lax.fori_loop(0, GROUP // 8, narrow, 0)
-
-    def copy(kind, part, i, partner):
-        channels = pl.ds(*PIECES[i])
+        lax.fori_loop(0, GROUP // 16, narrow, 0)
+
+    def copy(kind, part, source, target, partner):
         return pltpu.make_async_remote_copy(
-            src_ref=own.at[part, channels], dst_ref=columns.at[blk, part, channels],
-            send_sem=send_sems.at[kind, part], recv_sem=recv_sems.at[kind, part, i],
+            src_ref=source, dst_ref=target, send_sem=send_sems.at[kind], recv_sem=recv_sems.at[kind, part],
             device_id=partner, device_id_type=MESH,
         )
 
-    def arrived(kind, part, i):
-        copy(kind, part, i, to_pair).wait_recv()
-
-    def keep(part):
-        return [
-            pltpu.make_async_copy(own.at[part], columns.at[blk, part], keep_sems.at[0, part]),
-            pltpu.make_async_copy(own.at[part], rows.at[grid, part], keep_sems.at[1, part]),
-        ]
+    def arrived(kind, part):
+        copy(kind, part, own.at[part], columns.at[blk, part], to_pair).wait_recv()
+
+    def pass_on(kind, part, slot, start, stop, partner):
+        place = columns.at[slot, part, pl.ds(start, stop - start)]
+        copy(kind, part, place, place, partner).start()
+
+    def pass_last(part, slot, start, stop, partner):
+        place = columns.at[slot, part, pl.ds(start, stop - start)]
+        copy(PAIR_FAR, 0, place, place, partner).start()
 
     def first(part):
-        for i in (0, 2, 1, 3):
-            copy(PAIR, part, i, to_pair).start()
-            copy(UP, part, i, to_above).start()
-            copy(DOWN, part, i, to_below).start()
-        for local in keep(part):
-            local.start()
-
-    def pass_on(kind, part, i, slot, partner):
-        channels = pl.ds(*PIECES[i])
-        target = rows.at[grid, part, channels] if kind == ROW else columns.at[slot, part, channels]
-        pltpu.make_async_remote_copy(
-            src_ref=columns.at[slot, part, channels], dst_ref=target,
-            send_sem=send_sems.at[kind, part], recv_sem=recv_sems.at[kind, part, i],
-            device_id=partner, device_id_type=MESH,
-        ).start()
-
-    def pass_far(part, i):
-        if i % 2 == 0:
-            pass_on(FAR, part, i, below, to_above)
-        else:
-            pass_on(FAR, part, i, above, to_below)
+        copy(PAIR, part, own.at[part], columns.at[blk, part], to_pair).start()
+        copy(UP, part, own.at[part], columns.at[blk, part], to_above).start()
+        copy(DOWN, part, own.at[part], columns.at[blk, part], to_below).start()
 
     def second(part):
-        for i in (0, 2, 1, 3):
-            arrived(PAIR, part, i)
-            arrived(UP, part, i)
-            arrived(DOWN, part, i)
-            if i < 2:
-                pass_on(PAIR_UP, part, i, pair, to_above)
-                pass_on(PAIR_DOWN, part, i, pair, to_below)
-            else:
-                pass_on(PAIR_UP, part, i, below, to_pair)
-                pass_on(PAIR_DOWN, part, i, above, to_pair)
-            pass_far(part, i)
-            pass_on(ROW, part, i, pair, to_across)
+        arrived(UP, part)
+        pass_on(FAR, part, below, 0, GROUP // 2, to_above)
+        pass_on(PAIR_UP, part, below, SPLIT, GROUP, to_pair)
+        arrived(DOWN, part)
+        pass_on(FAR, part, above, GROUP // 2, GROUP, to_below)
+        pass_on(PAIR_DOWN, part, above, SPLIT, GROUP, to_pair)
+        arrived(PAIR, part)
+        pass_on(PAIR_UP, part, pair, 0, SPLIT, to_above)
+        pass_on(PAIR_DOWN, part, pair, 0, SPLIT, to_below)
+        copy(ROW, 0, columns.at[pair, part], rows.at[grid, part], to_across).start()
 
     def third(part):
-        for i in (2, 0, 3, 1):
-            arrived(FAR, part, i)
-            if i >= 2:
-                pass_on(PAIR_FAR, part, i, far, to_pair)
-            else:
-                arrived(PAIR_UP, part, i)
-                arrived(PAIR_DOWN, part, i)
-                if i == 0:
-                    pass_on(PAIR_FAR, part, i, pair_below, to_above)
-                else:
-                    pass_on(PAIR_FAR, part, i, pair_above, to_below)
-
-    def fourth(part):
-        for i in (2, 3):
-            arrived(PAIR_UP, part, i)
-            arrived(PAIR_DOWN, part, i)
-        for i in range(4):
-            arrived(PAIR_FAR, part, i)
-            arrived(ROW, part, i)
+        arrived(FAR, part)
+        pass_last(part, far, SPLIT, GROUP, to_pair)
+        arrived(PAIR_UP, part)
+        pass_last(part, pair_below, 0, SPLIT // 2, to_above)
+        arrived(PAIR_DOWN, part)
+        pass_last(part, pair_above, SPLIT // 2, SPLIT, to_below)
 
     turn_part(0)
     first(0)
@@ -328,28 +286,29 @@
     third(0)
     turn_part(3)
     first(3)
+    keeps = [
+        pltpu.make_async_copy(own, columns.at[blk], keep_sems.at[0]),
+        pltpu.make_async_copy(own, rows.at[grid], keep_sems.at[1]),
+    ]
+    for local in keeps:
+        local.start()
     second(2)
     third(1)
     second(3)
     third(2)
     third(3)
+    for local in keeps:
+        local.wait()
+
+    def whole(kind):
+        return copy(kind, 0, own, columns.at[blk], to_pair)
+
+    whole(PAIR_FAR).wait_recv()
+    whole(ROW).wait_recv()
+    for kind in range(8):
+        whole(kind).wait_send()
     for part in range(PARTS):
-        fourth(part)
-    for part in range(PARTS):
-        for local in keep(part):
-            local.wait()
-        for kind in range(8):
-            pltpu.make_async_remote_copy(
-                src_ref=own.at[part], dst_ref=columns.at[0, part], send_sem=send_sems.at[kind, part],
-                recv_sem=recv_sems.at[kind, part, 0], device_id=to_pair, device_id_type=MESH,
-            ).wait_send()
-
-    def drain(offset, carry):
-        for part in range(PARTS):
-            send(part, lax.rem(me + offset, SHARDS)).wait_send()
-        return carry
-
-    lax.fori_loop(1, SHARDS, drain, 0)
+        all_sent(part).wait_send()
 
 
 def gathered_spectra(samples, taps, chan_select):
@@ -366,7 +325,6 @@
         scratch_shapes=[
             pltpu.VMEM((INPUTS, HALO), BF16),
             pltpu.VMEM((PARTS * HEIGHT, FFT), BF16),
-            pltpu.VMEM((SHARDS // 2, FFT, 2 * LANES), BF16),
             pltpu.VMEM((256, 2 * LANES), F32),
             pltpu.VMEM((256, 2 * LANES), F32),
             pltpu.VMEM((PARTS, SHARDS, HEIGHT, LANES), BF16),
@@ -375,12 +333,13 @@
             pltpu.VMEM((GROUP * PART, 2 * DEPTH), F32),
             pltpu.VMEM(BLOCK, BF16),
             pltpu.SemaphoreType.DMA((2,)),
-            pltpu.SemaphoreType.DMA((PARTS, SHARDS)),
-            pltpu.SemaphoreType.DMA((PARTS, SHARDS)),
-            pltpu.SemaphoreType.DMA((2, PARTS)),
+            pltpu.SemaphoreType.DMA((PARTS,)),
+            pltpu.SemaphoreType.DMA((PARTS,)),
+            pltpu.SemaphoreType.DMA((2,)),
+            pltpu.SemaphoreType.DMA((8,)),
             pltpu.SemaphoreType.DMA((8, PARTS)),
-            pltpu.SemaphoreType.DMA((8, PARTS, len(PIECES))),
-        ],
+        ]
+        + [pltpu.VMEM((FFT, 2 * LANES), BF16)] * (SHARDS // 2),
         compiler_params=pltpu.CompilerParams(
             collective_id=0, has_side_effects=True, vmem_limit_bytes=VMEM_LIMIT
         ),
@@ -406,9 +365,8 @@
             early_and_late.append(jnp.stack(halves, 1).reshape(-1, 2 * DEPTH))
         return early_and_late
 
-    def multiply(i, carry):
-        for j in range(CHANNELS):
-            c = i * CHANNELS + j
+    for i in range(CHUNKS):
+        for c in range(i * CHANNELS, (i + 1) * CHANNELS):
             left = operand(rows, c)
             quarter = [jnp.concatenate([block[:, DEPTH:], block[:, :DEPTH]], 1) * sign for block in left]
             left = jnp.concatenate([jnp.concatenate(left, 1), jnp.concatenate(quarter, 1)], 0)
@@ -418,15 +376,8 @@
             ) * (1.0 / SPECTRA)
             products[:, c] = product.reshape(2, 2, INPUTS, 8 * INPUTS)
         store(i).start()
-        return carry
-
-    lax.fori_loop(0, CHUNKS, multiply, 0)
-
-    def finish(i, carry):
+    for i in range(CHUNKS):
         store(i).wait()
-        return carry
-
-    lax.fori_loop(0, CHUNKS, finish, 0)
 
 
 def cross_products(rows, columns):

time: 89.1 us -> 86.4 us (0.970)
  the two profiles are of different devices: /device:TPU:1 before, /device:TPU:8 now
where the time goes in v3:
time: 86.4 us; the launch traced here: 86.2 us
  Pallas kernels  83.6 us (97%)
  local copies, waits for them, and re-layouts  2.63 us (3%)
    pallas_call x1, Pallas kernels, gathered_spectra(): pl.pallas_call(spectra_kernel, out_shape=[jax.ShapeDtypeStruct((8,) + BLO...  79.7 us
    pallas_call x1, Pallas kernels, cross_products(): pl.pallas_call(cross_kernel, out_shape=jax.ShapeDtypeStruct(shape, F32),...  3.87 us
    unnamed x6, local copies, waits for them, and re-layouts  2.63 us

profile of v3, /device:TPU:8, one launch (start us, length us, event | category | flops | bytes accessed | tf_op | source)
XLA Modules:
  0.0 86.2 jit_solution(9985733921932208153)
XLA Ops:
  0.0 0.0 copy-start
  0.0 1.2 %copy-done = bf16[1,32,16384]{2,1,0:T(8,128)(2,1)S(1)} copy-done((bf16[1,32,16384]{2,1,0:T(8,128)(2,1)S(1)}, bf16[1,32,16384]{2,1,0:T(8,128)(2,1)}, u32[]{:S(2)}) %copy-start) | copy-done | bytes 1048600
  1.2 0.0 copy-start.1
  1.2 0.7 copy-done.1
  1.9 0.0 copy-start.2
  1.9 0.7 copy-done.2
  2.6 79.7 %spectra.1 = (bf16[8,4,64,16,128]{4,3,2,1,0:T(8,128)(2,1)S(1)}, bf16[2,4,64,16,128]{4,3,2,1,0:T(8,128)(2,1)S(1)}) custom-call(bf16[32,16384]{1,0:T(8,128)(2,1)S(1)} %bitcast.2, bf16[4,2048]{1,0:T(4,128)(2,1)S(1)} %copy-done.1, s32[8,128]{1,0:T(8,128)S(1)} %bitcast.3), custom_call_target="tpu_custom_call" | custom-call | tf_op jit(solution)/shard_map/spectra/pallas_call | solution.py:317
  82.4 3.9 %cross.1 = f32[2,64,2,32,256]{4,3,2,1,0:T(8,128)} custom-call(bf16[2,4,64,16,128]{4,3,2,1,0:T(8,128)(2,1)S(1)} %get-tuple-element.7.rows, bf16[8,4,64,16,128]{4,3,2,1,0:T(8,128)(2,1)S(1)} %get-tuple-element.8.columns), custom_call_target="tpu_custom_call" | custom-call | tf_op jit(solution)/shard_map/cross/pallas_call | solution.py:385
Async XLA Ops:
  0.0 1.2 %copy-start = (bf16[1,32,16384]{2,1,0:T(8,128)(2,1)S(1)}, bf16[1,32,16384]{2,1,0:T(8,128)(2,1)}, u32[]{:S(2)}) copy-start(bf16[1,32,16384]{2,1,0:T(8,128)(2,1)} %param.3) | copy-start | bytes 3145732
  1.2 0.7 copy-start.1
  1.9 0.7 copy-start.2

commit v4 on v3

--- a/solution.py
+++ b/solution.py
@@ -183,9 +183,9 @@
         device_id={"chan": lax.rem(me + 1, SHARDS)},
         device_id_type=MESH,
     )
-    halo.start()
     for i in range(len(chips)):
         leave(1, i)
+    halo.start()
 
     def early_frames():
         halo.wait_send()
@@ -276,13 +276,13 @@
 
     turn_part(0)
     first(0)
-    early_frames()
     turn_part(1)
     first(1)
     second(0)
+    early_frames()
+    second(1)
     turn_part(2)
     first(2)
-    second(1)
     third(0)
     turn_part(3)
     first(3)
@@ -292,8 +292,8 @@
     ]
     for local in keeps:
         local.start()
+    third(1)
     second(2)
-    third(1)
     second(3)
     third(2)
     third(3)

time: 86.4 us -> 82.7 us (0.957)
  the two profiles are of different devices: /device:TPU:8 before, /device:TPU:1 now
where the time goes in v4:
time: 82.7 us; the launch traced here: 82.5 us
  Pallas kernels  79.9 us (97%)
  local copies, waits for them, and re-layouts  2.63 us (3%)
    pallas_call x1, Pallas kernels, gathered_spectra(): pl.pallas_call(spectra_kernel, out_shape=[jax.ShapeDtypeStruct((8,) + BLO...  76 us
    pallas_call x1, Pallas kernels, cross_products(): pl.pallas_call(cross_kernel, out_shape=jax.ShapeDtypeStruct(shape, F32),...  3.88 us
    unnamed x6, local copies, waits for them, and re-layouts  2.63 us

profile of v4, /device:TPU:1, one launch (start us, length us, event | category | flops | bytes accessed | tf_op | source)
XLA Modules:
  0.0 82.5 jit_solution(14390754725527024905)
XLA Ops:
  0.0 0.0 copy-start
  0.0 1.2 %copy-done = bf16[1,32,16384]{2,1,0:T(8,128)(2,1)S(1)} copy-done((bf16[1,32,16384]{2,1,0:T(8,128)(2,1)S(1)}, bf16[1,32,16384]{2,1,0:T(8,128)(2,1)}, u32[]{:S(2)}) %copy-start) | copy-done | bytes 1048600
  1.2 0.0 copy-start.1
  1.2 0.7 copy-done.1
  1.9 0.0 copy-start.2
  1.9 0.7 copy-done.2
  2.6 76.0 %spectra.1 = (bf16[8,4,64,16,128]{4,3,2,1,0:T(8,128)(2,1)S(1)}, bf16[2,4,64,16,128]{4,3,2,1,0:T(8,128)(2,1)S(1)}) custom-call(bf16[32,16384]{1,0:T(8,128)(2,1)S(1)} %bitcast.2, bf16[4,2048]{1,0:T(4,128)(2,1)S(1)} %copy-done.1, s32[8,128]{1,0:T(8,128)S(1)} %bitcast.3), custom_call_target="tpu_custom_call" | custom-call | tf_op jit(solution)/shard_map/spectra/pallas_call | solution.py:317
  78.6 3.9 %cross.1 = f32[2,64,2,32,256]{4,3,2,1,0:T(8,128)} custom-call(bf16[2,4,64,16,128]{4,3,2,1,0:T(8,128)(2,1)S(1)} %get-tuple-element.7.rows, bf16[8,4,64,16,128]{4,3,2,1,0:T(8,128)(2,1)S(1)} %get-tuple-element.8.columns), custom_call_target="tpu_custom_call" | custom-call | tf_op jit(solution)/shard_map/cross/pallas_call | solution.py:385
Async XLA Ops:
  0.0 1.2 %copy-start = (bf16[1,32,16384]{2,1,0:T(8,128)(2,1)S(1)}, bf16[1,32,16384]{2,1,0:T(8,128)(2,1)}, u32[]{:S(2)}) copy-start(bf16[1,32,16384]{2,1,0:T(8,128)(2,1)} %param.3) | copy-start | bytes 3145732
  1.2 0.7 copy-start.1
  1.9 0.7 copy-start.2

commit v5 on v4

--- a/solution.py
+++ b/solution.py
@@ -30,7 +30,7 @@
 HEIGHT = STEPS * PART
 DEPTH = SHARDS * STEPS
 BLOCK = (PARTS, GROUP, PART, 2 * DEPTH)
-SPLIT = 36
+SPLIT = 35
 PAIR, UP, DOWN, FAR, PAIR_UP, PAIR_DOWN, PAIR_FAR, ROW = range(8)
 
 
@@ -50,7 +50,7 @@
 
 
 def spectra_kernel(
-    samples, taps, chan_select, columns, rows, history, filt, fine_cos, fine_sin, sent, landed,
+    samples, taps, chan_select, columns, rows, history, filt, sent, landed,
     spread, turned, own, halo_sems, turn_send, turn_recv, keep_sems, send_sems, recv_sems, *tables,
 ):
     me = lax.axis_index("chan")
@@ -151,12 +151,11 @@
         sin_v = jnp.concatenate([both[1] for both in fine], 0)
         for u in range(MIDDLE):
             cos_u, sin_u = (t[u % 8 : u % 8 + 1] for t in middle[u // 8])
-            fine_cos[pl.ds(u * FINE, FINE), :] = cos_u * cos_v - sin_u * sin_v
-            fine_sin[pl.ds(u * FINE, FINE), :] = sin_u * cos_v + cos_u * sin_v
-        for p in range(COARSE):
-            place = pl.ds(p * 256, 256)
-            turned_on = cos_p[p : p + 1] * fine_cos[...] - sin_p[p : p + 1] * fine_sin[...]
-            table[place, :] = turned_on.astype(BF16)
+            fine_cos = cos_u * cos_v - sin_u * sin_v
+            fine_sin = sin_u * cos_v + cos_u * sin_v
+            for p in range(COARSE):
+                turned_on = cos_p[p : p + 1] * fine_cos - sin_p[p : p + 1] * fine_sin
+                table[pl.ds(p * 256 + u * FINE, FINE), :] = turned_on.astype(BF16)
 
     def transform(early, i):
         to_z = chips[i]
@@ -207,11 +206,12 @@
         all_sent(part).wait_recv()
 
         def widen(i, carry):
-            place = pl.ds(pl.multiple_of(i * 4 * HEIGHT, 4 * HEIGHT), 4 * HEIGHT)
+            place = pl.ds(i * 4 * HEIGHT, 4 * HEIGHT)
             spread[place, :] = landed[part, pl.ds(i * 4, 4)].astype(F32).reshape(4 * HEIGHT, LANES)
             return carry
 
-        lax.fori_loop(0, SHARDS // 4, widen, 0)
+        for k in range(SHARDS // 4):
+            widen(k, 0)
         low = lax.broadcasted_iota(jnp.int32, (GROUP, 2 * DEPTH), 1) < DEPTH
 
         def turn(k, carry):
@@ -223,14 +223,16 @@
                 turned[pl.ds(a + 1, GROUP, stride=PART), :] = jnp.where(low, pltpu.roll(real, DEPTH, 1), imag)
             return carry
 
-        lax.fori_loop(0, PART // 4, turn, 0)
+        for k in range(PART // 4):
+            turn(k, 0)
 
         def narrow(c, carry):
-            place = pl.ds(pl.multiple_of(c * 16 * PART, 16 * PART), 16 * PART)
+            place = pl.ds(c * 16 * PART, 16 * PART)
             own[part, pl.ds(c * 16, 16)] = turned[place, :].astype(BF16).reshape(16, PART, 2 * DEPTH)
             return carry
 
-        lax.fori_loop(0, GROUP // 16, narrow, 0)
+        for k in range(GROUP // 16):
+            narrow(k, 0)
 
     def copy(kind, part, source, target, partner):
         return pltpu.make_async_remote_copy(
@@ -250,9 +252,9 @@
         copy(PAIR_FAR, 0, place, place, partner).start()
 
     def first(part):
-        copy(PAIR, part, own.at[part], columns.at[blk, part], to_pair).start()
         copy(UP, part, own.at[part], columns.at[blk, part], to_above).start()
         copy(DOWN, part, own.at[part], columns.at[blk, part], to_below).start()
+        copy(PAIR, part, own.at[part], columns.at[blk, part], to_pair).start()
 
     def second(part):
         arrived(UP, part)
@@ -270,9 +272,9 @@
         arrived(FAR, part)
         pass_last(part, far, SPLIT, GROUP, to_pair)
         arrived(PAIR_UP, part)
-        pass_last(part, pair_below, 0, SPLIT // 2, to_above)
+        pass_last(part, pair_below, 0, (SPLIT // 2 + 1), to_above)
         arrived(PAIR_DOWN, part)
-        pass_last(part, pair_above, SPLIT // 2, SPLIT, to_below)
+        pass_last(part, pair_above, (SPLIT // 2 + 1), SPLIT, to_below)
 
     turn_part(0)
     first(0)
@@ -325,8 +327,6 @@
         scratch_shapes=[
             pltpu.VMEM((INPUTS, HALO), BF16),
             pltpu.VMEM((PARTS * HEIGHT, FFT), BF16),
-            pltpu.VMEM((256, 2 * LANES), F32),
-            pltpu.VMEM((256, 2 * LANES), F32),
             pltpu.VMEM((PARTS, SHARDS, HEIGHT, LANES), BF16),
             pltpu.VMEM((PARTS, SHARDS, HEIGHT, LANES), BF16),
             pltpu.VMEM((SHARDS * HEIGHT, LANES), F32),

time: 82.7 us -> 81.8 us (0.989)
  Pallas kernels: 79.9 us -> 78.9 us
    pallas_call x1, Pallas kernels: 76 us -> 75 us  [gathered_spectra(): pl.pallas_call(spectra_kernel, out_shape=[jax.ShapeDtypeStruct((8,) + BLO...]
where the time goes in v5:
time: 81.8 us; the launch traced here: 81.6 us
  Pallas kernels  78.9 us (96%)
  local copies, waits for them, and re-layouts  2.63 us (3%)
    pallas_call x1, Pallas kernels, gathered_spectra(): pl.pallas_call(spectra_kernel, out_shape=[jax.ShapeDtypeStruct((8,) + BLO...  75 us
    pallas_call x1, Pallas kernels, cross_products(): pl.pallas_call(cross_kernel, out_shape=jax.ShapeDtypeStruct(shape, F32),...  3.88 us
    unnamed x6, local copies, waits for them, and re-layouts  2.63 us

profile of v5, /device:TPU:1, one launch (start us, length us, event | category | flops | bytes accessed | tf_op | source)
XLA Modules:
  0.0 81.6 jit_solution(1228118175054582001)
XLA Ops:
  0.0 0.0 copy-start
  0.0 1.2 %copy-done = bf16[1,32,16384]{2,1,0:T(8,128)(2,1)S(1)} copy-done((bf16[1,32,16384]{2,1,0:T(8,128)(2,1)S(1)}, bf16[1,32,16384]{2,1,0:T(8,128)(2,1)}, u32[]{:S(2)}) %copy-start) | copy-done | bytes 1048600
  1.2 0.0 copy-start.1
  1.2 0.7 copy-done.1
  1.9 0.0 copy-start.2
  1.9 0.7 copy-done.2
  2.6 75.0 %spectra.1 = (bf16[8,4,64,16,128]{4,3,2,1,0:T(8,128)(2,1)S(1)}, bf16[2,4,64,16,128]{4,3,2,1,0:T(8,128)(2,1)S(1)}) custom-call(bf16[32,16384]{1,0:T(8,128)(2,1)S(1)} %bitcast.2, bf16[4,2048]{1,0:T(4,128)(2,1)S(1)} %copy-done.1, s32[8,128]{1,0:T(8,128)S(1)} %bitcast.3), custom_call_target="tpu_custom_call" | custom-call | tf_op jit(solution)/shard_map/spectra/pallas_call | solution.py:319
  77.7 3.9 %cross.1 = f32[2,64,2,32,256]{4,3,2,1,0:T(8,128)} custom-call(bf16[2,4,64,16,128]{4,3,2,1,0:T(8,128)(2,1)S(1)} %get-tuple-element.7.rows, bf16[8,4,64,16,128]{4,3,2,1,0:T(8,128)(2,1)S(1)} %get-tuple-element.8.columns), custom_call_target="tpu_custom_call" | custom-call | tf_op jit(solution)/shard_map/cross/pallas_call | solution.py:385
Async XLA Ops:
  0.0 1.2 %copy-start = (bf16[1,32,16384]{2,1,0:T(8,128)(2,1)S(1)}, bf16[1,32,16384]{2,1,0:T(8,128)(2,1)}, u32[]{:S(2)}) copy-start(bf16[1,32,16384]{2,1,0:T(8,128)(2,1)} %param.3) | copy-start | bytes 3145732
  1.2 0.7 copy-start.1
  1.9 0.7 copy-start.2

commit v6 on v5

--- a/solution.py
+++ b/solution.py
@@ -74,7 +74,8 @@
         pl.semaphore_signal(barrier, inc=1, device_id={"chan": lax.rem(me + offset, SHARDS)}, device_id_type=MESH)
         return carry
 
-    lax.fori_loop(1, SHARDS, greet, 0)
+    for offset in range(1, SHARDS):
+        greet(offset, 0)
     for partner in (to_pair, to_below, to_above, to_across):
         pl.semaphore_signal(barrier, inc=1, device_id=partner, device_id_type=MESH)
 
@@ -85,7 +86,7 @@
             s = step + STEPS * (1 - early)
 
             def part(i, carry):
-                lanes = pl.multiple_of(i * width, width)
+                lanes = i * width
                 total = jnp.zeros((INPUTS, width), F32)
                 for t in range(TAPS):
                     weight = taps[pl.ds(t, 1), pl.ds(lanes, width)].astype(F32)
@@ -101,7 +102,8 @@
                     filt[place, pl.ds(lanes, width)] = total[half * PART : (half + 1) * PART]
                 return carry
 
-            lax.fori_loop(0, FFT // width, part, 0)
+            for i in range(FFT // width):
+                part(i, 0)
 
     filter_frames(0)
     pl.semaphore_wait(barrier, SHARDS - 1 + 4)

time: 81.8 us -> 81.9 us (level)
  no operation moved by 1% of the time
where the time goes in v6:
time: 81.9 us; the launch traced here: 81.7 us
  Pallas kernels  78.9 us (96%)
  local copies, waits for them, and re-layouts  2.63 us (3%)
    pallas_call x1, Pallas kernels, gathered_spectra(): pl.pallas_call(spectra_kernel, out_shape=[jax.ShapeDtypeStruct((8,) + BLO...  75 us
    pallas_call x1, Pallas kernels, cross_products(): pl.pallas_call(cross_kernel, out_shape=jax.ShapeDtypeStruct(shape, F32),...  3.88 us
    unnamed x6, local copies, waits for them, and re-layouts  2.63 us

profile of v6, /device:TPU:1, one launch (start us, length us, event | category | flops | bytes accessed | tf_op | source)
XLA Modules:
  0.0 81.7 jit_solution(18348303157281280305)
XLA Ops:
  0.0 0.0 copy-start
  0.0 1.2 %copy-done = bf16[1,32,16384]{2,1,0:T(8,128)(2,1)S(1)} copy-done((bf16[1,32,16384]{2,1,0:T(8,128)(2,1)S(1)}, bf16[1,32,16384]{2,1,0:T(8,128)(2,1)}, u32[]{:S(2)}) %copy-start) | copy-done | bytes 1048600
  1.2 0.0 copy-start.1
  1.2 0.7 copy-done.1
  1.9 0.0 copy-start.2
  1.9 0.7 copy-done.2
  2.6 75.0 %spectra.1 = (bf16[8,4,64,16,128]{4,3,2,1,0:T(8,128)(2,1)S(1)}, bf16[2,4,64,16,128]{4,3,2,1,0:T(8,128)(2,1)S(1)}) custom-call(bf16[32,16384]{1,0:T(8,128)(2,1)S(1)} %bitcast.2, bf16[4,2048]{1,0:T(4,128)(2,1)S(1)} %copy-done.1, s32[8,128]{1,0:T(8,128)S(1)} %bitcast.3), custom_call_target="tpu_custom_call" | custom-call | tf_op jit(solution)/shard_map/spectra/pallas_call | solution.py:321
  77.7 3.9 %cross.1 = f32[2,64,2,32,256]{4,3,2,1,0:T(8,128)} custom-call(bf16[2,4,64,16,128]{4,3,2,1,0:T(8,128)(2,1)S(1)} %get-tuple-element.7.rows, bf16[8,4,64,16,128]{4,3,2,1,0:T(8,128)(2,1)S(1)} %get-tuple-element.8.columns), custom_call_target="tpu_custom_call" | custom-call | tf_op jit(solution)/shard_map/cross/pallas_call | solution.py:387
Async XLA Ops:
  0.0 1.2 %copy-start = (bf16[1,32,16384]{2,1,0:T(8,128)(2,1)S(1)}, bf16[1,32,16384]{2,1,0:T(8,128)(2,1)}, u32[]{:S(2)}) copy-start(bf16[1,32,16384]{2,1,0:T(8,128)(2,1)} %param.3) | copy-start | bytes 3145732
  1.2 0.7 copy-start.1
  1.9 0.7 copy-start.2
